TPU v7x, 512 devices: a whole 4x8x8 slice. The times are simulated.
512 devices in a mesh: grad: 32 (over y, z_hi), dp: 16 (over x, z_lo, core).
Axes of the slice: x: 4, y: 8, z: 8 (z_hi: 4, z_lo: 2; z = z_hi * 2 + z_lo), core: 2. Of those that a mesh axis runs over, the one named last changes fastest.
Arguments:
- gradient: bfloat16 [32, 512, 5120], P('grad', 'dp'), may hold values from -6 to 6
- out_bases: bfloat16 [32, 512, 512], P('grad'), may hold values from -0.25 to 0.25
- in_bases: bfloat16 [32, 512, 512], P('grad'), may hold values from -0.25 to 0.25
- out_values: float32 [32, 512], P('grad'), may hold values from 0.3 to 3
- in_values: float32 [2, 5120], replicated, may hold values from 0.3 to 3
- block_layer: int32 [32], P('grad'), may hold values from 0 to 1
- in_owner: int32 [2, 10], replicated, may hold values from 0 to 31, as said below
Outputs:
- preconditioned: bfloat16 [32, 512, 5120], P('grad', 'dp')
Inputs may be any that keep to these rules, and one draw needn't show every extreme that they name: `in_owner`: entries are distinct; entry (l, j) names slot s of the stored bases, held by gradient worker s // 1 as its local slot s % 1.
All inputs are finite; a program needn't handle non-finite values.
Results may differ from a plain program's by a relative error of at most 0.0055.
Values may be sent and summed in bfloat16 or wider, within the bound.
A program may use at most 64 MiB of HBM per device.

v0:
```python
import jax
import jax.numpy as jnp
from jax import lax
from jax.sharding import PartitionSpec as P

DAMPING = 0.1


def spread(shard, axis, root):
    mine = lax.axis_index(axis) == root
    return lax.psum(jnp.where(mine, shard, jnp.zeros_like(shard)), axis)


def right_product(rows_data, layer_tiles):
    slot_count, row_count, full_width = rows_data.shape
    block_count = layer_tiles.shape[1]
    block_size = layer_tiles.shape[2]
    blocked = rows_data.reshape(slot_count, row_count, block_count, block_size)
    projected = jnp.einsum(
        "srjk,sjkc->srjc", blocked, layer_tiles, preferred_element_type=jnp.float32
    )
    return projected.astype(jnp.bfloat16).reshape(slot_count, row_count, full_width)


def back_product(rows_data, layer_tiles):
    slot_count, row_count, full_width = rows_data.shape
    block_count = layer_tiles.shape[1]
    block_size = layer_tiles.shape[2]
    blocked = rows_data.reshape(slot_count, row_count, block_count, block_size)
    result = jnp.einsum("srjc,sjkc->srjk", blocked, layer_tiles, preferred_element_type=jnp.float32)
    return result.astype(jnp.bfloat16).reshape(slot_count, row_count, full_width)


def scale_columns(out_bases, columns, out_values, value_cols):
    moments = jnp.einsum("sra,src->sac", out_bases, columns, preferred_element_type=jnp.float32)
    scaled = (moments / (out_values[:, :, None] * value_cols[:, None, :] + DAMPING)).astype(
        jnp.bfloat16
    )
    mixed_cols = jnp.einsum("sra,sac->src", out_bases, scaled, preferred_element_type=jnp.float32)
    return mixed_cols.astype(jnp.bfloat16)


def shards(gradient, out_bases, in_bases, out_values, in_values, block_layer, in_owner):
    held_slots = in_bases.shape[0]
    block_size = in_bases.shape[1]
    layer_count = in_owner.shape[0]
    block_count = in_owner.shape[1]
    peer_count = lax.axis_size("dp")
    peer_index = lax.axis_index("dp")
    tiles_list = []
    for layer_index in range(layer_count):
        for block_index in range(block_count):
            owner_slot = in_owner[layer_index, block_index]
            basis_tile = lax.dynamic_index_in_dim(
                in_bases, owner_slot % held_slots, 0, keepdims=False
            )
            tiles_list.append(spread(basis_tile, "grad", owner_slot // held_slots))
    in_tiles = jnp.stack(tiles_list).reshape(layer_count, block_count, block_size, block_size)
    layer_tiles = jnp.take(in_tiles, block_layer, axis=0)
    projected = right_product(gradient, layer_tiles)
    col_width = gradient.shape[2] // peer_count
    layer_values = jnp.take(in_values, block_layer, axis=0)
    value_cols = lax.dynamic_slice_in_dim(layer_values, peer_index * col_width, col_width, 1)
    columns = lax.all_to_all(projected, "dp", split_axis=2, concat_axis=1, tiled=True)
    mixed_cols = scale_columns(out_bases, columns, out_values, value_cols)
    returned = lax.all_to_all(mixed_cols, "dp", split_axis=1, concat_axis=2, tiled=True)
    return back_product(returned, layer_tiles)


def solution(mesh):
    in_specs = (
        P("grad", "dp", None),
        P("grad", None, None),
        P("grad", None, None),
        P("grad", None),
        P(),
        P("grad"),
        P(),
    )
    out_specs = P("grad", "dp", None)
    return jax.shard_map(shards, mesh=mesh, in_specs=in_specs, out_specs=out_specs, check_vma=False)
```

profile of v0, /device:TPU:1, one launch (start us, length us, event | category | flops | bytes accessed | tf_op | source)
XLA Modules:
  0.0 670.9 jit_solution(15815527690538584883)
XLA Ops:
  6.5 0.0 copy-start
  6.5 0.0 all-reduce.3.cloned.1.call-start
  6.5 2.1 fusion.36
  8.6 1.3 slice.78
  22.5 2.1 broadcast_select_fusion.1
  24.6 4.7 broadcast_select_fusion
  29.3 0.0 all-reduce.3.cloned.1.call-update
  30.0 0.2 reshape.130
  30.2 534.5 %all-reduce.3.cloned.1.call-done = (bf16[1,512,512]{2,1,0:T(8,128)(2,1)}, bf16[1,512,512]{2,1,0:T(8,128)(2,1)}, bf16[1,512,512]{2,1,0:T(8,128)(2,1)}, bf16[1,512...) async-done(((bf16[1,512,512]{2,1,0:T(8,128)(2,1)}, ...) | async-done | bytes 10485776 | tf_op jit(solution)/shard_map/psum | solution.py:11
  564.8 1.2 constant_dynamic-update-slice_fusion.19
  566.0 1.5 constant_dynamic-update-slice_fusion.18
  567.5 1.1 constant_dynamic-update-slice_fusion.17
  568.6 1.1 constant_dynamic-update-slice_fusion.16
  569.7 1.1 constant_dynamic-update-slice_fusion.15
  570.7 1.1 constant_dynamic-update-slice_fusion.14
  571.8 1.1 constant_dynamic-update-slice_fusion.13
  572.9 1.1 constant_dynamic-update-slice_fusion.12
  574.0 1.1 constant_dynamic-update-slice_fusion.11
  575.1 1.1 constant_dynamic-update-slice_fusion.10
  576.2 0.0 copy-done.9
  576.3 0.0 copy-done.7
  576.4 0.0 copy-done.5
  576.5 0.0 copy-done.3
  576.6 0.0 copy-done.1
  576.7 1.3 fusion.18
  578.0 2.7 copy-done.12
  580.7 1.8 copy.26
  582.5 0.5 broadcast.191
  583.0 28.9 %reduce.2 = bf16[5120,32]{1,0:T(8,128)(2,1)} reduce(bf16[5120,1,32]{2,1,0:T(2,128)(2,1)S(1)} %bitcast.77, bf16[]{:T(256)} %broadcast.191), dimensions={1}, to_apply=%bitcast.72.reduce_sub_computation | reduce | bytes 655362
  611.9 3.4 reshape.206
  615.4 14.6 %all-to-all-start = ((bf16[16,2,5120]{2,1,0:T(2,128)(2,1)}), bf16[16,2,5120]{2,1,0:T(2,128)(2,1)S(1)}, u32[]{:S(2)}, u32[]{:S(2)}) async-start(bf16[16,2,5120]{2,1,0:T(2,128)(2,1)} %reshape.206), calls=%async_computation | async-start | bytes 655360 | tf_op jit(solution)/shard_map/all_to_all | solution.py:64
  629.9 0.8 fusion.30
  630.7 6.9 %all-to-all-done = bf16[16,2,5120]{2,1,0:T(2,128)(2,1)S(1)} async-done(((bf16[16,2,5120]{2,1,0:T(2,128)(2,1)}), bf16[16,2,5120]{2,1,0:T(2,128)(2,1)S(1)}, u32[]{:S(2)}, u32[]{:S(2)}) %all-to-all-start) | async-done | bytes 327712 | tf_op jit(solution)/shard_map/all_to_all | solution.py:64
  637.6 1.5 reshape.207
  639.2 1.4 copy.27
  640.6 0.3 all_to_all.23
  640.9 0.1 copy.28
  641.0 0.6 fusion.14
  641.6 1.2 copy.29
  642.8 3.1 reduce.3
  645.9 0.4 reshape.208
  646.4 11.4 %all_to_all.30 = bf16[16,2,5120]{2,1,0:T(2,128)(2,1)S(1)} all-to-all(bf16[16,2,5120]{2,1,0:T(2,128)(2,1)S(1)} %reshape.208), channel_id=1, replica_groups=mesh['grad'=32,'dp'=16] {'dp'}, dimensions={0} | all-to-all | bytes 655360 | tf_op jit(solution)/shard_map/all_to_all | solution.py:66
  657.7 0.7 reshape.209
  658.4 0.1 copy.33
  658.5 0.1 copy.30
  658.6 0.6 reshape.134
  659.2 4.1 fusion.15
  663.3 0.8 copy.35
  (32 shorter events, 0.4 us)
Async XLA Ops:
  6.5 634.4 %copy-start = (bf16[1,512,512]{2,1,0:T(8,128)(2,1)S(1)}, bf16[1,512,512]{2,1,0:T(8,128)(2,1)}, u32[]{:S(2)}) copy-start(bf16[1,512,512]{2,1,0:T(8,128)(2,1)} %param.8) | copy-start | bytes 1572868
  6.5 558.2 %all-reduce.3.cloned.1.call-start = ((), (), s32[]{:S(2)}) async-start(), calls=%async_computation.2 | async-start | bytes 20971520 | tf_op jit(solution)/shard_map/psum | solution.py:11
  24.6 5.3 copy-start.11
  564.7 11.5 %copy-start.10 = (bf16[1,512,512]{2,1,0:T(8,128)(2,1)S(1)}, bf16[1,512,512]{2,1,0:T(8,128)(2,1)}, u32[]{:S(2)}) copy-start(bf16[1,512,512]{2,1,0:T(8,128)(2,1)} %get-tuple-element.37) | copy-start | bytes 1572868
  564.7 11.5 %copy-start.9 = (bf16[1,512,512]{2,1,0:T(8,128)(2,1)S(1)}, bf16[1,512,512]{2,1,0:T(8,128)(2,1)}, u32[]{:S(2)}) copy-start(bf16[1,512,512]{2,1,0:T(8,128)(2,1)} %get-tuple-element.38) | copy-start | bytes 1572868
  564.7 11.6 %copy-start.8 = (bf16[1,512,512]{2,1,0:T(8,128)(2,1)S(1)}, bf16[1,512,512]{2,1,0:T(8,128)(2,1)}, u32[]{:S(2)}) copy-start(bf16[1,512,512]{2,1,0:T(8,128)(2,1)} %get-tuple-element.39) | copy-start | bytes 1572868
  564.7 11.6 %copy-start.7 = (bf16[1,512,512]{2,1,0:T(8,128)(2,1)S(1)}, bf16[1,512,512]{2,1,0:T(8,128)(2,1)}, u32[]{:S(2)}) copy-start(bf16[1,512,512]{2,1,0:T(8,128)(2,1)} %get-tuple-element.40) | copy-start | bytes 1572868
  564.7 11.7 %copy-start.6 = (bf16[1,512,512]{2,1,0:T(8,128)(2,1)S(1)}, bf16[1,512,512]{2,1,0:T(8,128)(2,1)}, u32[]{:S(2)}) copy-start(bf16[1,512,512]{2,1,0:T(8,128)(2,1)} %get-tuple-element.41) | copy-start | bytes 1572868
  564.7 11.7 %copy-start.5 = (bf16[1,512,512]{2,1,0:T(8,128)(2,1)S(1)}, bf16[1,512,512]{2,1,0:T(8,128)(2,1)}, u32[]{:S(2)}) copy-start(bf16[1,512,512]{2,1,0:T(8,128)(2,1)} %get-tuple-element.42) | copy-start | bytes 1572868
  564.7 11.8 %copy-start.4 = (bf16[1,512,512]{2,1,0:T(8,128)(2,1)S(1)}, bf16[1,512,512]{2,1,0:T(8,128)(2,1)}, u32[]{:S(2)}) copy-start(bf16[1,512,512]{2,1,0:T(8,128)(2,1)} %get-tuple-element.43) | copy-start | bytes 1572868
  564.7 11.8 %copy-start.3 = (bf16[1,512,512]{2,1,0:T(8,128)(2,1)S(1)}, bf16[1,512,512]{2,1,0:T(8,128)(2,1)}, u32[]{:S(2)}) copy-start(bf16[1,512,512]{2,1,0:T(8,128)(2,1)} %get-tuple-element.44) | copy-start | bytes 1572868
  564.7 11.8 %copy-start.2 = (bf16[1,512,512]{2,1,0:T(8,128)(2,1)S(1)}, bf16[1,512,512]{2,1,0:T(8,128)(2,1)}, u32[]{:S(2)}) copy-start(bf16[1,512,512]{2,1,0:T(8,128)(2,1)} %get-tuple-element.45) | copy-start | bytes 1572868
  564.8 11.9 %copy-start.1 = (bf16[1,512,512]{2,1,0:T(8,128)(2,1)S(1)}, bf16[1,512,512]{2,1,0:T(8,128)(2,1)}, u32[]{:S(2)}) copy-start(bf16[1,512,512]{2,1,0:T(8,128)(2,1)} %get-tuple-element.46) | copy-start | bytes 1572868
  576.7 4.0 copy-start.12
  578.0 63.0 %copy-start.13 = (f32[1,512]{1,0:T(1,128)S(1)}, f32[1,512]{1,0:T(1,128)}, u32[]{:S(2)}) copy-start(f32[1,512]{1,0:T(1,128)} %param.10) | copy-start | bytes 6148
  615.4 22.3 %all-to-all-start = ((bf16[16,2,5120]{2,1,0:T(2,128)(2,1)}), bf16[16,2,5120]{2,1,0:T(2,128)(2,1)S(1)}, u32[]{:S(2)}, u32[]{:S(2)}) async-start(bf16[16,2,5120]{2,1,0:T(2,128)(2,1)} %reshape.206), calls=%async_computation | async-start | bytes 655360 | tf_op jit(solution)/shard_map/all_to_all | solution.py:64
Sparse Core Ops, SparseCore 0:
  29.4 535.2 all-reduce.2
where the time goes:
time: 672 us; the launch traced here: 671 us
  waiting for transfers between devices  541 us (81%)
  other arithmetic  39.6 us (6%)
  local copies, waits for them, and re-layouts  30.9 us (5%)
  between operations  27 us (4%)
  starting transfers between devices  14.6 us (2%)
  blocking collectives  11.4 us (2%)
    psum x1, waiting for transfers between devices, spread(): return lax.psum(jnp.where(mine, shard, jnp.zeros_like(shard)), axis)  535 us
    unnamed x2, other arithmetic  32.1 us
    unnamed x53, local copies, waits for them, and re-layouts  21.1 us
    all_to_all x1, starting transfers between devices, shards(): lax.all_to_all(projected, 'dp', split_axis=2, concat_axis=1, tiled=True)  14.6 us
  transfers between devices with their start and end apart: 2, of which 2 were waited for; matrix products, arithmetic and copies ran while one was open for 0% of the time, Pallas kernels for 0%

commit v1 on v0

v1 whole, which is shorter than its diff:
```python
import jax
import jax.numpy as jnp
from jax import lax
from jax.experimental import pallas as pl
from jax.experimental.pallas import tpu as pltpu
from jax.sharding import PartitionSpec as P

DAMPING = 0.1
MESH = pl.DeviceIdType.MESH
ZN = 4
RIGHT, LEFT = 0, 1


def owner_device(j):
    return jnp.where(j < 8, 2 * j, jnp.where(j == 8, 1, 11))


def owned_block(p):
    return jnp.where(p % 2 == 0, p // 2, jnp.where(p == 1, 8, 9))


def hops(direction, k):
    if direction == RIGHT:
        return 4 if k < 2 else 3
    return 3 if k < 2 else 4


def dot(a, b, contract):
    return lax.dot_general(a, b, (contract, ((), ())), preferred_element_type=jnp.float32)


def kernel(
    yn, pn, jn,
    owner_ref, layer_ref, grad_ref, ob_ref, ib_ref, ov_ref, iv_ref,
    out_ref,
    obuf, obt, gbuf, ybuf, rbuf, tall, tsend, tbuf, sbuf, res,
    lsem, zs, zr, ys, yr, gs, gr, ts, tr, ms, mr,
):
    g = lax.axis_index("grad")
    p = lax.axis_index("dp")
    y, zh = g // ZN, g % ZN
    rows = grad_ref.shape[1]
    blk = ob_ref.shape[1]
    own_rows = pl.ds(pl.multiple_of(p * rows, rows), rows)
    active = (p % 2 == 0) | (p == 1) | (p == 11)
    mine = owned_block(p)

    def remote(src, dst, ssem, rsem, gg, pp):
        return pltpu.make_async_remote_copy(
            src_ref=src, dst_ref=dst, send_sem=ssem, recv_sem=rsem, device_id=(gg, pp), device_id_type=MESH
        )

    def slot(yy, k):
        return lax.rem(yy + 2 * yn, yn) * ZN + lax.rem(zh - k + ZN, ZN)

    load_basis = pltpu.make_async_copy(ob_ref.at[0], obuf, lsem.at[0])
    load_strip = pltpu.make_async_copy(ib_ref.at[0, own_rows, :], tall.at[g], lsem.at[1])
    load_basis.start()
    load_strip.start()

    zpeer = [y * ZN + lax.rem(zh + k, ZN) for k in range(ZN)]
    ypeer = (lax.rem(y + 1, yn) * ZN + zh, lax.rem(y + yn - 1, yn) * ZN + zh)

    barrier = pltpu.get_barrier_semaphore()
    for i in range(1, pn):
        pl.semaphore_signal(barrier, inc=1, device_id=(g, lax.rem(p + i, pn)), device_id_type=MESH)
    for k in range(1, ZN):
        pl.semaphore_signal(barrier, inc=1, device_id=(zpeer[k], p), device_id_type=MESH)
    for d in (RIGHT, LEFT):
        pl.semaphore_signal(barrier, inc=1, device_id=(ypeer[d], p), device_id_type=MESH)
    pl.semaphore_wait(barrier, pn - 1 + ZN - 1 + 2)

    zcopy = {}
    for k in (1, 3, 2):
        zcopy[k] = remote(ib_ref.at[0, own_rows, :], tall.at[g], zs.at[k - 1], zr.at[k - 1], zpeer[k], p)
        zcopy[k].start()

    def ycopy(d, hop, k):
        origin = y - hop if d == RIGHT else y + hop
        s = slot(origin, k)
        src = ib_ref.at[0, own_rows, :] if hop == 0 and k == 0 else tall.at[s]
        return remote(src, tall.at[s], ys.at[d, hop, k], yr.at[d, hop, k], ypeer[d], p)

    for d in (RIGHT, LEFT):
        ycopy(d, 0, 0).start()

    def gcopy(i):
        j = lax.rem(i + p, jn)
        return j, remote(
            grad_ref.at[0, :, pl.ds(pl.multiple_of(j * blk, blk), blk)],
            gbuf.at[own_rows, :], gs.at[i], gr, g, owner_device(j),
        )

    for i in range(jn):
        j, copy = gcopy(i)

        @pl.when(owner_device(j) != p)
        def _():
            copy.start()

    @pl.when(active)
    def _():
        pltpu.make_async_copy(
            grad_ref.at[0, :, pl.ds(pl.multiple_of(mine * blk, blk), blk)], gbuf.at[own_rows, :], gr
        ).start()

    layer = layer_ref[0]
    load_basis.wait()

    @pl.when(active)
    def _():
        obt[...] = obuf[...].T
        spread = jnp.broadcast_to(ov_ref[...], (128, blk)).T
        for c in range(0, blk, 128):
            values = iv_ref[:, pl.ds(pl.multiple_of(mine * blk + c, 128), 128)]
            values = jnp.where(layer == 0, values[0:1], values[1:2])
            rbuf[:, c : c + 128] = 1.0 / (spread * values + DAMPING)

    load_strip.wait()
    for k in (1, 3, 2):
        zcopy[k].wait_recv()
        for d in (RIGHT, LEFT):
            ycopy(d, 0, k).start()

    def project(lo, size):
        @pl.when(active)
        def _():
            if lo == 0:
                pltpu.make_async_copy(gbuf, gbuf, gr).wait()
            ybuf[lo : lo + size, :] = dot(obt[lo : lo + size, :], gbuf[...], ((1,), (0,))).astype(jnp.bfloat16)

    order = (0, 1, 3, 2)
    for hop in range(1, 5):
        for n, k in enumerate(order):
            for d in (RIGHT, LEFT):
                if hop <= hops(d, k):
                    ycopy(d, hop - 1, k).wait_recv()
                    if hop < hops(d, k):
                        ycopy(d, hop, k).start()
            if hop == 2:
                project(n * (blk // 4), blk // 4)

    def tcopy(i):
        j = lax.rem(i + p, jn)
        return j, remote(tsend.at[j], tbuf.at[own_rows, :], ts.at[i], tr, g, owner_device(j))

    for i in range(jn):
        j, copy = tcopy(i)
        tsend[j] = tall[owner_ref[layer, j]]

        @pl.when(owner_device(j) != p)
        def _():
            copy.start()

    def mcopy(i, base):
        dest = base + i
        strip = pl.ds(pl.multiple_of(dest * rows, rows), rows)
        cols = pl.ds(pl.multiple_of(mine * blk, blk), blk)
        return dest, res.at[strip, :], out_ref.at[0, :, cols]

    half = blk // 2
    per_half = pn // 2

    @pl.when(active)
    def _():
        pltpu.make_async_copy(tsend.at[mine], tbuf.at[own_rows, :], tr).start()
        pltpu.make_async_copy(tbuf, tbuf, tr).wait()
        for lo in (0, half):
            moments = dot(ybuf[lo : lo + half, :], tbuf[...], ((1,), (0,)))
            sbuf[lo : lo + half, :] = (moments * rbuf[lo : lo + half, :]).astype(jnp.bfloat16)
        for lo in (0, 1):
            part = slice(lo * half, lo * half + half)
            mixed = dot(obuf[part, :], sbuf[...], ((1,), (0,))).astype(jnp.bfloat16)
            res[part, :] = dot(mixed, tbuf[...], ((1,), (1,))).astype(jnp.bfloat16)
            for i in range(per_half):
                dest, src, dst = mcopy(i, lo * per_half)

                @pl.when(dest != p)
                def _():
                    remote(src, dst, ms.at[dest], mr, g, dest).start()

                @pl.when(dest == p)
                def _():
                    pltpu.make_async_copy(src, dst, mr).start()

    pltpu.make_async_copy(out_ref.at[0], out_ref.at[0], mr).wait()

    for k in (1, 3, 2):
        zcopy[k].wait_send()
    for d in (RIGHT, LEFT):
        for k in range(ZN):
            for hop in range(hops(d, k)):
                ycopy(d, hop, k).wait_send()
    for i in range(jn):
        j, copy = gcopy(i)
        _, other = tcopy(i)

        @pl.when(owner_device(j) != p)
        def _():
            copy.wait_send()
            other.wait_send()

    @pl.when(active)
    def _():
        for i in range(pn):
            dest, src, dst = mcopy(i, 0)

            @pl.when(dest != p)
            def _():
                remote(src, dst, ms.at[dest], mr, g, dest).wait_send()


def solution(mesh):
    yn = mesh.shape["grad"] // ZN
    pn = mesh.shape["dp"]

    def shards(gradient, out_bases, in_bases, out_values, in_values, block_layer, in_owner):
        rows, width = gradient.shape[1:]
        blk = out_bases.shape[1]
        jn = width // blk
        slots = yn * ZN
        bf16, f32 = jnp.bfloat16, jnp.float32
        any_spec = pl.BlockSpec(memory_space=pl.ANY)
        smem = pl.BlockSpec(memory_space=pltpu.SMEM)
        vmem = pl.BlockSpec(memory_space=pltpu.VMEM)
        dma = pltpu.SemaphoreType.DMA

        def body(*refs):
            kernel(yn, pn, jn, *refs)

        return pl.pallas_call(
            body,
            out_shape=jax.ShapeDtypeStruct(gradient.shape, bf16),
            in_specs=[smem, smem, any_spec, any_spec, any_spec, vmem, vmem],
            out_specs=any_spec,
            scratch_shapes=[
                pltpu.VMEM((blk, blk), bf16),
                pltpu.VMEM((blk, blk), bf16),
                pltpu.VMEM((blk, blk), bf16),
                pltpu.VMEM((blk, blk), bf16),
                pltpu.VMEM((blk, blk), f32),
                pltpu.VMEM((slots, rows, blk), bf16),
                pltpu.VMEM((jn, rows, blk), bf16),
                pltpu.VMEM((blk, blk), bf16),
                pltpu.VMEM((blk, blk), bf16),
                pltpu.VMEM((blk, blk), bf16),
                dma((2,)),
                dma((ZN - 1,)),
                dma((ZN - 1,)),
                dma((2, 4, ZN)),
                dma((2, 4, ZN)),
                dma((jn,)),
                dma,
                dma((jn,)),
                dma,
                dma((pn,)),
                dma,
            ],
            compiler_params=pltpu.CompilerParams(
                collective_id=0, has_side_effects=True, vmem_limit_bytes=32 * 1024 * 1024
            ),
        )(in_owner, block_layer, gradient, out_bases, in_bases, out_values, in_values)

    in_specs = (
        P("grad", "dp", None),
        P("grad", None, None),
        P("grad", None, None),
        P("grad", None),
        P(),
        P("grad"),
        P(),
    )
    return jax.shard_map(shards, mesh=mesh, in_specs=in_specs, out_specs=P("grad", "dp", None), check_vma=False)
```

time: 672 us -> 54 us (0.08)
  waiting for transfers between devices: 541 us -> 0 us
  Pallas kernels: 0 us -> 47.7 us
  other arithmetic: 39.6 us -> 0 us
  between operations: 27 us -> 0.69 us
  local copies, waits for them, and re-layouts: 30.9 us -> 5.25 us
  starting transfers between devices: 14.6 us -> 0 us
  blocking collectives: 11.4 us -> 0 us
    psum x1 -> x0, waiting for transfers between devices: 535 us -> none  [spread(): return lax.psum(jnp.where(mine, shard, jnp.zeros_like(shard)), axis)]
    pallas_call x0 -> x1, Pallas kernels: none -> 47.7 us  [shards(): pl.pallas_call(body, out_shape=jax.ShapeDtypeStruct(gradient.shape, bf16)...]
    unnamed x2 -> x0, other arithmetic: 32.1 us -> none
    unnamed x53 -> x13, local copies, waits for them, and re-layouts: 21.1 us -> 5.25 us
    all_to_all x1 -> x0, starting transfers between devices: 14.6 us -> none  [shards(): lax.all_to_all(projected, 'dp', split_axis=2, concat_axis=1, tiled=True)]
    all_to_all x1 -> x0, blocking collectives: 11.4 us -> none  [shards(): lax.all_to_all(mixed_cols, 'dp', split_axis=1, concat_axis=2, tiled=True)]
    all_to_all x1 -> x0, waiting for transfers between devices: 6.9 us -> none  [shards(): lax.all_to_all(projected, 'dp', split_axis=2, concat_axis=1, tiled=True)]
    select_n x2 -> x0, other arithmetic: 6.77 us -> none  [spread(): return lax.psum(jnp.where(mine, shard, jnp.zeros_like(shard)), axis)]
  transfers between devices with their start and end apart: 2 -> 0, of which waited for: 2 -> 0; matrix products, arithmetic and copies ran while one was open for 0% -> 0% of each run, Pallas kernels for 0% -> 0%
where the time goes in v1:
time: 54 us; the launch traced here: 53.6 us
  Pallas kernels  47.7 us (88%)
  local copies, waits for them, and re-layouts  5.25 us (10%)
  between operations  0.69 us (1%)
    pallas_call x1, Pallas kernels, shards(): pl.pallas_call(body, out_shape=jax.ShapeDtypeStruct(gradient.shape, bf16)...  47.7 us
    unnamed x13, local copies, waits for them, and re-layouts  5.25 us

profile of v1, /device:TPU:1, one launch (start us, length us, event | category | flops | bytes accessed | tf_op | source)
XLA Modules:
  0.0 53.6 jit_solution(7270731854212239286)
XLA Ops:
  0.0 0.0 copy-start.5
  0.7 0.0 copy-done.5
  0.7 0.0 copy-start
  0.7 1.0 %copy-done = bf16[1,512,512]{2,1,0:T(8,128)(2,1)S(1)} copy-done((bf16[1,512,512]{2,1,0:T(8,128)(2,1)S(1)}, bf16[1,512,512]{2,1,0:T(8,128)(2,1)}, u32[]{:S(2)}) %copy-start) | copy-done | bytes 524312
  1.7 0.0 copy-start.1
  1.7 1.0 %copy-done.1 = bf16[1,512,512]{2,1,0:T(8,128)(2,1)S(1)} copy-done((bf16[1,512,512]{2,1,0:T(8,128)(2,1)S(1)}, bf16[1,512,512]{2,1,0:T(8,128)(2,1)}, u32[]{:S(2)}) %copy-start.1) | copy-done | bytes 524312
  2.8 0.0 copy-start.2
  2.8 1.0 %copy-done.2 = bf16[1,32,5120]{2,1,0:T(8,128)(2,1)S(1)} copy-done((bf16[1,32,5120]{2,1,0:T(8,128)(2,1)S(1)}, bf16[1,32,5120]{2,1,0:T(8,128)(2,1)}, u32[]{:S(2)}) %copy-start.2) | copy-done | bytes 327704
  3.7 0.0 copy-start.3
  3.7 0.8 %copy-done.3 = f32[2,5120]{1,0:T(2,128)S(1)} copy-done((f32[2,5120]{1,0:T(2,128)S(1)}, f32[2,5120]{1,0:T(2,128)}, u32[]{:S(2)}) %copy-start.3) | copy-done | bytes 40984
  4.5 0.0 copy-start.4
  4.5 0.7 %copy-done.4 = f32[1,512]{1,0:T(1,128)S(1)} copy-done((f32[1,512]{1,0:T(1,128)S(1)}, f32[1,512]{1,0:T(1,128)}, u32[]{:S(2)}) %copy-start.4) | copy-done | bytes 2072
  5.2 47.7 %shard_map.73 = bf16[1,32,5120]{2,1,0:T(8,128)(2,1)S(1)} custom-call(s32[2,10]{1,0:T(2,128)S(1)} %copy-done.5, s32[1]{0:T(128)S(6)} %copy.9.refs_1_, bf16[1,32,5120]{2,1,0:T(8,128)(2,1)S(1)} %copy-done.2, bf16[1,512,512]{2,1,0:T(8,128)(2,1)S(1)} %copy-done, bf16[1,512,512]{2,1,0:T(8,128)(2,1)S(1)} %copy-done.1, f32[1,512]{1,0:T(1,128)S(1)} %copy-done.4, ...), custom_call_target="tpu_custom_call" | custom-call | tf_op jit(solution)/shard_map/pallas_call | solution.py:231
  52.9 0.7 %copy.10 = bf16[1,32,5120]{2,1,0:T(8,128)(2,1)} copy(bf16[1,32,5120]{2,1,0:T(8,128)(2,1)S(1)} %shard_map.73) | data formatting | bytes 655360
Async XLA Ops:
  0.0 0.7 %copy-start.5 = (s32[2,10]{1,0:T(2,128)S(1)}, s32[2,10]{1,0:T(2,128)}, u32[]{:S(2)}) copy-start(s32[2,10]{1,0:T(2,128)} %refs_0_.1) | copy-start | bytes 244
  0.7 1.0 %copy-start = (bf16[1,512,512]{2,1,0:T(8,128)(2,1)S(1)}, bf16[1,512,512]{2,1,0:T(8,128)(2,1)}, u32[]{:S(2)}) copy-start(bf16[1,512,512]{2,1,0:T(8,128)(2,1)} %refs_3_.1) | copy-start | bytes 1572868
  1.7 1.0 %copy-start.1 = (bf16[1,512,512]{2,1,0:T(8,128)(2,1)S(1)}, bf16[1,512,512]{2,1,0:T(8,128)(2,1)}, u32[]{:S(2)}) copy-start(bf16[1,512,512]{2,1,0:T(8,128)(2,1)} %refs_4_.1) | copy-start | bytes 1572868
  2.8 1.0 %copy-start.2 = (bf16[1,32,5120]{2,1,0:T(8,128)(2,1)S(1)}, bf16[1,32,5120]{2,1,0:T(8,128)(2,1)}, u32[]{:S(2)}) copy-start(bf16[1,32,5120]{2,1,0:T(8,128)(2,1)} %refs_2_.1) | copy-start | bytes 983044
  3.7 0.8 %copy-start.3 = (f32[2,5120]{1,0:T(2,128)S(1)}, f32[2,5120]{1,0:T(2,128)}, u32[]{:S(2)}) copy-start(f32[2,5120]{1,0:T(2,128)} %refs_6_.1) | copy-start | bytes 122884
  4.5 0.7 %copy-start.4 = (f32[1,512]{1,0:T(1,128)S(1)}, f32[1,512]{1,0:T(1,128)}, u32[]{:S(2)}) copy-start(f32[1,512]{1,0:T(1,128)} %refs_5_.1) | copy-start | bytes 6148

commit v2 on v1

--- a/solution.py
+++ b/solution.py
@@ -9,6 +9,13 @@
 MESH = pl.DeviceIdType.MESH
 ZN = 4
 RIGHT, LEFT = 0, 1
+SCHEME = ("skip", "skip", "skip", "skip")
+ORDER = (
+    ("y", 0, 1), ("prepare", 0), ("up", 1, "first"), ("y", 0, 2), ("prepare", 1), ("z", 1), ("up", 1, "rest"),
+    ("up", 2, "all"), ("up", 3, "all"), ("prepare", 2), ("y", 0, 3), ("prepare", 3), ("y", 0, 4), ("z", 2), ("z", 3),
+    ("y", 1, 1), ("y", 1, 2), ("project", 0), ("y", 2, 1), ("y", 2, 2), ("project", 1), ("y", 3, 1), ("y", 3, 2),
+    ("project", 2), ("y", 1, 3), ("y", 1, 4), ("project", 3), ("y", 2, 3), ("y", 2, 4), ("y", 3, 3), ("y", 3, 4),
+)
 
 
 def owner_device(j):
@@ -19,10 +26,12 @@
     return jnp.where(p % 2 == 0, p // 2, jnp.where(p == 1, 8, 9))
 
 
-def hops(direction, k):
-    if direction == RIGHT:
-        return 4 if k < 2 else 3
-    return 3 if k < 2 else 4
+def reach(direction, c):
+    return 4 if (c < 2) == (direction == RIGHT) else 3
+
+
+def eval_where(which, zh):
+    return zh % 2 == 0 if which == "first" else zh % 2 == 1 if which == "rest" else True
 
 
 def dot(a, b, contract):
@@ -31,10 +40,10 @@
 
 def kernel(
     yn, pn, jn,
-    owner_ref, layer_ref, grad_ref, ob_ref, ib_ref, ov_ref, iv_ref,
+    owner_in, layer_in, grad_ref, ob_ref, ib_ref, ov_ref, iv_ref,
     out_ref,
-    obuf, obt, gbuf, ybuf, rbuf, tall, tsend, tbuf, sbuf, res,
-    lsem, zs, zr, ys, yr, gs, gr, ts, tr, ms, mr,
+    owner_ref, layer_ref, obuf, obt, gbuf, ybuf, rbuf, tall, tsend, tbuf, sbuf, res,
+    lsem, zready, zs, zr, ys, yr, gs, gr, ts, tr, ms, mr,
 ):
     g = lax.axis_index("grad")
     p = lax.axis_index("dp")
@@ -50,39 +59,84 @@
             src_ref=src, dst_ref=dst, send_sem=ssem, recv_sem=rsem, device_id=(gg, pp), device_id_type=MESH
         )
 
-    def slot(yy, k):
-        return lax.rem(yy + 2 * yn, yn) * ZN + lax.rem(zh - k + ZN, ZN)
-
-    load_basis = pltpu.make_async_copy(ob_ref.at[0], obuf, lsem.at[0])
-    load_strip = pltpu.make_async_copy(ib_ref.at[0, own_rows, :], tall.at[g], lsem.at[1])
-    load_basis.start()
-    load_strip.start()
-
-    zpeer = [y * ZN + lax.rem(zh + k, ZN) for k in range(ZN)]
-    ypeer = (lax.rem(y + 1, yn) * ZN + zh, lax.rem(y + yn - 1, yn) * ZN + zh)
+    def zpeer(k):
+        return y * ZN + lax.rem(zh + k + ZN, ZN)
+
+    def ypeer(d):
+        return lax.rem(y + d + yn, yn) * ZN + zh
+
+    def slot(d, k):
+        return lax.rem(y + d + yn, yn) * ZN + lax.rem(zh - k + ZN, ZN)
+
+    loads = [
+        pltpu.make_async_copy(src, dst, lsem.at[i])
+        for i, (src, dst) in enumerate(
+            ((ib_ref.at[0, own_rows, :], tall.at[g]), (ob_ref.at[0], obuf), (owner_in, owner_ref), (layer_in, layer_ref))
+        )
+    ]
+    load_strip, load_basis, load_owner, load_layer = loads
+    for load in loads:
+        load.start()
 
     barrier = pltpu.get_barrier_semaphore()
+    for k in (3, 2, 1):
+        @pl.when(zh + k < ZN)
+        def _():
+            pl.semaphore_signal(barrier, inc=1, device_id=(zpeer(k), p), device_id_type=MESH)
+    for d in (1, -1, 2, -2):
+        pl.semaphore_signal(barrier, inc=1, device_id=(ypeer(d), p), device_id_type=MESH)
     for i in range(1, pn):
         pl.semaphore_signal(barrier, inc=1, device_id=(g, lax.rem(p + i, pn)), device_id_type=MESH)
-    for k in range(1, ZN):
-        pl.semaphore_signal(barrier, inc=1, device_id=(zpeer[k], p), device_id_type=MESH)
-    for d in (RIGHT, LEFT):
-        pl.semaphore_signal(barrier, inc=1, device_id=(ypeer[d], p), device_id_type=MESH)
-    pl.semaphore_wait(barrier, pn - 1 + ZN - 1 + 2)
-
-    zcopy = {}
+    pl.semaphore_wait(barrier, pn - 1 + 4 + zh)
+    for k in (1, 2, 3):
+        @pl.when(zh - k >= 0)
+        def _():
+            pl.semaphore_signal(zready.at[k - 1], inc=1, device_id=(zpeer(-k), p), device_id_type=MESH)
+
+    def zcopy(k):
+        return remote(ib_ref.at[0, own_rows, :], tall.at[g], zs.at[k - 1], zr.at[k - 1], zpeer(k), p)
+
+    def zup(k, where=True):
+        @pl.when((zh + k < ZN) & where)
+        def _():
+            pl.semaphore_wait(zready.at[k - 1], 1)
+            zcopy(k).start()
+
     for k in (1, 3, 2):
-        zcopy[k] = remote(ib_ref.at[0, own_rows, :], tall.at[g], zs.at[k - 1], zr.at[k - 1], zpeer[k], p)
-        zcopy[k].start()
-
-    def ycopy(d, hop, k):
-        origin = y - hop if d == RIGHT else y + hop
-        s = slot(origin, k)
-        src = ib_ref.at[0, own_rows, :] if hop == 0 and k == 0 else tall.at[s]
-        return remote(src, tall.at[s], ys.at[d, hop, k], yr.at[d, hop, k], ypeer[d], p)
-
-    for d in (RIGHT, LEFT):
-        ycopy(d, 0, 0).start()
+        @pl.when(zh + k >= ZN)
+        def _():
+            zcopy(k).start()
+
+    first = jnp.where(zh % 2 == 0, 3, 1)
+    kinds = (0, first, 4 - first, 2)
+
+    def ycopy(d, c, here, there):
+        sign = 1 if d == RIGHT else -1
+        s = slot(-sign * here, kinds[c])
+        src = ib_ref.at[0, own_rows, :] if here == 0 and c == 0 else tall.at[s]
+        return remote(src, tall.at[s], ys.at[d, there - 1, c], yr.at[d, there - 1, c], ypeer(sign * (there - here)), p)
+
+    def onward(c, here):
+        for d in (RIGHT, LEFT):
+            for there in range(here + 1, reach(d, c) + 1):
+                if SCHEME[c] == "chain":
+                    go = there == here + 1
+                else:
+                    go = here in (0, 2) and there <= here + 2
+                if go:
+                    ycopy(d, c, here, there).start()
+
+    def zgot(c):
+        pltpu.make_async_copy(tall.at[0], tall.at[0], zr.at[kinds[c] - 1]).wait()
+        onward(c, 0)
+
+    def ygot(c, here):
+        for d in (RIGHT, LEFT):
+            if here <= reach(d, c):
+                pltpu.make_async_copy(tall.at[0], tall.at[0], yr.at[d, here - 1, c]).wait()
+        onward(c, here)
+
+    onward(0, 0)
 
     def gcopy(i):
         j = lax.rem(i + p, jn)
@@ -104,41 +158,44 @@
             grad_ref.at[0, :, pl.ds(pl.multiple_of(mine * blk, blk), blk)], gbuf.at[own_rows, :], gr
         ).start()
 
+    load_layer.wait()
+    load_owner.wait()
+    load_strip.wait()
+    load_basis.wait()
     layer = layer_ref[0]
-    load_basis.wait()
-
-    @pl.when(active)
-    def _():
-        obt[...] = obuf[...].T
-        spread = jnp.broadcast_to(ov_ref[...], (128, blk)).T
-        for c in range(0, blk, 128):
-            values = iv_ref[:, pl.ds(pl.multiple_of(mine * blk + c, 128), 128)]
+
+    def prepare(n):
+        part = slice(n * (blk // 4), (n + 1) * (blk // 4))
+
+        @pl.when(active)
+        def _():
+            obt[:, part] = obuf[part, :].T
+            spread = jnp.broadcast_to(ov_ref[...], (blk // 4, blk)).T
+            values = iv_ref[:, pl.ds(pl.multiple_of(mine * blk + n * (blk // 4), blk // 4), blk // 4)]
             values = jnp.where(layer == 0, values[0:1], values[1:2])
-            rbuf[:, c : c + 128] = 1.0 / (spread * values + DAMPING)
-
-    load_strip.wait()
-    for k in (1, 3, 2):
-        zcopy[k].wait_recv()
-        for d in (RIGHT, LEFT):
-            ycopy(d, 0, k).start()
-
-    def project(lo, size):
+            rbuf[:, part] = 1.0 / (spread * values + DAMPING)
+
+    def project(n):
+        lo, size = n * (blk // 4), blk // 4
+
         @pl.when(active)
         def _():
             if lo == 0:
                 pltpu.make_async_copy(gbuf, gbuf, gr).wait()
             ybuf[lo : lo + size, :] = dot(obt[lo : lo + size, :], gbuf[...], ((1,), (0,))).astype(jnp.bfloat16)
 
-    order = (0, 1, 3, 2)
-    for hop in range(1, 5):
-        for n, k in enumerate(order):
-            for d in (RIGHT, LEFT):
-                if hop <= hops(d, k):
-                    ycopy(d, hop - 1, k).wait_recv()
-                    if hop < hops(d, k):
-                        ycopy(d, hop, k).start()
-            if hop == 2:
-                project(n * (blk // 4), blk // 4)
+    for step in ORDER:
+        what, n = step[0], step[1]
+        if what == "up":
+            zup(n, eval_where(step[2], zh))
+        elif what == "z":
+            zgot(n)
+        elif what == "y":
+            ygot(n, step[2])
+        elif what == "prepare":
+            prepare(n)
+        else:
+            project(n)
 
     def tcopy(i):
         j = lax.rem(i + p, jn)
@@ -185,12 +242,12 @@
 
     pltpu.make_async_copy(out_ref.at[0], out_ref.at[0], mr).wait()
 
-    for k in (1, 3, 2):
-        zcopy[k].wait_send()
+    for k in (1, 2, 3):
+        zcopy(k).wait_send()
     for d in (RIGHT, LEFT):
-        for k in range(ZN):
-            for hop in range(hops(d, k)):
-                ycopy(d, hop, k).wait_send()
+        for c in range(ZN):
+            for there in range(1, reach(d, c) + 1):
+                pltpu.make_async_copy(tall.at[0], tall.at[0], ys.at[d, there - 1, c]).wait()
     for i in range(jn):
         j, copy = gcopy(i)
         _, other = tcopy(i)
@@ -221,7 +278,6 @@
         slots = yn * ZN
         bf16, f32 = jnp.bfloat16, jnp.float32
         any_spec = pl.BlockSpec(memory_space=pl.ANY)
-        smem = pl.BlockSpec(memory_space=pltpu.SMEM)
         vmem = pl.BlockSpec(memory_space=pltpu.VMEM)
         dma = pltpu.SemaphoreType.DMA
 
@@ -230,10 +286,12 @@
 
         return pl.pallas_call(
             body,
-            out_shape=jax.ShapeDtypeStruct(gradient.shape, bf16),
-            in_specs=[smem, smem, any_spec, any_spec, any_spec, vmem, vmem],
-            out_specs=any_spec,
+            out_shape=pltpu.VMEM(gradient.shape, bf16),
+            in_specs=[any_spec] * 5 + [vmem] * 2,
+            out_specs=vmem,
             scratch_shapes=[
+                pltpu.SMEM(in_owner.shape, jnp.int32),
+                pltpu.SMEM(block_layer.shape, jnp.int32),
                 pltpu.VMEM((blk, blk), bf16),
                 pltpu.VMEM((blk, blk), bf16),
                 pltpu.VMEM((blk, blk), bf16),
@@ -244,7 +302,8 @@
                 pltpu.VMEM((blk, blk), bf16),
                 pltpu.VMEM((blk, blk), bf16),
                 pltpu.VMEM((blk, blk), bf16),
-                dma((2,)),
+                dma((4,)),
+                pltpu.SemaphoreType.REGULAR((ZN - 1,)),
                 dma((ZN - 1,)),
                 dma((ZN - 1,)),
                 dma((2, 4, ZN)),
@@ -257,7 +316,7 @@
                 dma,
             ],
             compiler_params=pltpu.CompilerParams(
-                collective_id=0, has_side_effects=True, vmem_limit_bytes=32 * 1024 * 1024
+                collective_id=0, has_side_effects=True, vmem_limit_bytes=60 * 1024 * 1024
             ),
         )(in_owner, block_layer, gradient, out_bases, in_bases, out_values, in_values)
 

time: 54 us -> 47.8 us (0.89)
  local copies, waits for them, and re-layouts: 5.25 us -> 0.73 us
  Pallas kernels: 47.7 us -> 45.9 us
    unnamed x13 -> x1, local copies, waits for them, and re-layouts: 5.25 us -> 0.73 us
    pallas_call x1, Pallas kernels: 47.7 us -> 45.9 us  [shards(): pl.pallas_call(body, out_shape=pltpu.VMEM(gradient.shape, bf16), in_specs...]
where the time goes in v2:
time: 47.8 us; the launch traced here: 47.3 us
  Pallas kernels  45.9 us (96%)
  local copies, waits for them, and re-layouts  0.73 us (2%)
  between operations  0.66 us (1%)
    pallas_call x1, Pallas kernels, shards(): pl.pallas_call(body, out_shape=pltpu.VMEM(gradient.shape, bf16), in_specs...  45.9 us

profile of v2, /device:TPU:1, one launch (start us, length us, event | category | flops | bytes accessed | tf_op | source)
XLA Modules:
  0.0 47.3 jit_solution(12700084718522560056)
XLA Ops:
  0.7 45.9 %shard_map.73 = bf16[1,32,5120]{2,1,0:T(8,128)(2,1)S(1)} custom-call(s32[2,10]{1,0:T(2,128)} %refs_0_.1, s32[1]{0:T(128)S(6)} %copy.10.refs_1_, bf16[1,32,5120]{2,1,0:T(8,128)(2,1)} %refs_2_.1, bf16[1,512,512]{2,1,0:T(8,128)(2,1)} %refs_3_.1, bf16[1,512,512]{2,1,0:T(8,128)(2,1)} %refs_4_.1, f32[1,512]{1,0:T(1,128)} %refs_5_.1, f32[2,5120]{1,0:T(2,128)} %refs_6_.1), custom_call_target="tpu_custom_call" | custom-call | tf_op jit(solution)/shard_map/pallas_call | solution.py:287
  46.6 0.7 %copy.9 = bf16[1,32,5120]{2,1,0:T(8,128)(2,1)} copy(bf16[1,32,5120]{2,1,0:T(8,128)(2,1)S(1)} %shard_map.73) | data formatting | bytes 655360

commit v3 on v2

v3 whole, which is shorter than its diff:
```python
import jax
import jax.numpy as jnp
from jax import lax
from jax.experimental import pallas as pl
from jax.experimental.pallas import tpu as pltpu
from jax.sharding import PartitionSpec as P

DAMPING = 0.1
MESH = pl.DeviceIdType.MESH
ZN = 4
RIGHT, LEFT = 0, 1
UPPER, LOWER = 0, 1
ORDER = (
    ("y", 0, 1, LOWER), ("y", 0, 1, UPPER), ("up", 1, "first"), ("y", 0, 2, LOWER), ("bundle", "down"), ("y", 0, 2, UPPER),
    ("prepare", 0), ("prepare", 1),
    ("z", 1, UPPER), ("up", 1, "rest"), ("up", 2, "all"), ("up", 3, "all"), ("bundle", "up"), ("prepare", 2), ("prepare", 3),

    ("z", 2, UPPER), ("z", 3, UPPER), ("z", 3, LOWER), ("y", 0, 3, LOWER), ("y", 0, 4, LOWER), ("bundle", "far"),
    ("y", 1, 1, UPPER), ("y", 1, 2, UPPER), ("y", 2, 1, UPPER), ("y", 2, 2, UPPER), ("y", 3, 1, UPPER), ("y", 3, 2, UPPER),
    ("y", 3, 1, LOWER), ("y", 3, 2, LOWER),
    ("y", 0, 3, UPPER), ("y", 0, 4, UPPER), ("y", 1, 3, UPPER), ("y", 1, 4, UPPER),
    ("y", 2, 3, UPPER), ("y", 2, 4, UPPER), ("y", 3, 3, UPPER), ("y", 3, 4, UPPER),
    ("owners", UPPER),
    ("z", 1, LOWER), ("z", 2, LOWER), ("bundled", 1), ("bundled", 3), ("y", 3, 3, LOWER), ("y", 3, 4, LOWER),
    ("owners", LOWER), ("project", 0), ("project", 1), ("project", 2), ("project", 3),
)


def owner_device(j):
    return jnp.where(j < 8, 2 * j + 1, jnp.where(j == 8, 0, 10))


def turn(i, p):
    if i < 4:
        n = lax.rem(i + p // 2, 4)
        return jnp.where(n == 0, 0, jnp.where(n == 1, 5, 6 + n))
    n = lax.rem(i - 4 + p // 2, 6)
    return jnp.where(n < 4, n + 1, n + 2)


def owned_block(p):
    return jnp.where(p % 2 == 1, p // 2, jnp.where(p == 0, 8, 9))


def reach(direction, c, h):
    return 4 if ((c == 1) if c in (1, 2) else (h == UPPER)) == (direction == RIGHT) else 3


def eval_where(which, zh):
    return zh % 2 == 0 if which == "first" else zh % 2 == 1 if which == "rest" else True


def dot(a, b, contract):
    return lax.dot_general(a, b, (contract, ((), ())), preferred_element_type=jnp.float32)


def kernel(
    yn, pn, jn,
    owner_in, layer_in, grad_ref, ob_ref, ib_ref, ov_ref, iv_ref,
    out_ref,
    owner_ref, layer_ref, obuf, obt, gbuf, ybuf, rbuf, tall_u, tall_l, tsend_u, tsend_l, tbuf, sbuf, res,
    lsem, zready, zs, zr, bs, br, ys, yr, gs, gr, ts, tr, ms, mr,
):
    g = lax.axis_index("grad")
    p = lax.axis_index("dp")
    y, zh = g // ZN, g % ZN
    rows = grad_ref.shape[1]
    blk = ob_ref.shape[1]
    part = rows // 2
    own_rows = pl.ds(pl.multiple_of(p * rows, rows), rows)
    tall, tsend = (tall_u, tall_l), (tsend_u, tsend_l)

    def half_rows(h):
        return pl.ds(pl.multiple_of(p * rows + h * part, part), part)
    active = (p % 2 == 1) | (p == 0) | (p == 10)
    mine = owned_block(p)

    def remote(src, dst, ssem, rsem, gg, pp):
        return pltpu.make_async_remote_copy(
            src_ref=src, dst_ref=dst, send_sem=ssem, recv_sem=rsem, device_id=(gg, pp), device_id_type=MESH
        )

    def zpeer(k):
        return y * ZN + lax.rem(zh + k + ZN, ZN)

    def ypeer(d):
        return lax.rem(y + d + yn, yn) * ZN + zh

    def slot(d, k):
        return lax.rem(y + d + yn, yn) * ZN + lax.rem(zh - k + ZN, ZN)

    loads = [
        pltpu.make_async_copy(src, dst, lsem.at[i])
        for i, (src, dst) in enumerate(
            (
                (ib_ref.at[0, half_rows(UPPER), :], tall_u.at[g]), (ib_ref.at[0, half_rows(LOWER), :], tall_l.at[g]),
                (ob_ref.at[0], obuf), (owner_in, owner_ref), (layer_in, layer_ref),
            )
        )
    ]
    for load in loads:
        load.start()

    barrier = pltpu.get_barrier_semaphore()
    for k in (3, 2, 1):
        @pl.when(zh + k < ZN)
        def _():
            pl.semaphore_signal(barrier, inc=1, device_id=(zpeer(k), p), device_id_type=MESH)
    for d in (1, -1, 2, -2):
        pl.semaphore_signal(barrier, inc=1, device_id=(ypeer(d), p), device_id_type=MESH)
    for i in range(1, pn):
        pl.semaphore_signal(barrier, inc=1, device_id=(g, lax.rem(p + i, pn)), device_id_type=MESH)
    pl.semaphore_wait(barrier, pn - 1 + 4 + zh)
    for k in (1, 2, 3):
        @pl.when(zh - k >= 0)
        def _():
            pl.semaphore_signal(zready.at[k - 1], inc=1, device_id=(zpeer(-k), p), device_id_type=MESH)

    for load in loads[:2]:
        load.wait()

    def zcopy(k, h):
        return remote(
            tall[h].at[g], tall[h].at[g], zs.at[k - 1, h], zr.at[k - 1, h], zpeer(k), p
        )

    def zup(k, where=True):
        @pl.when((zh + k < ZN) & where)
        def _():
            pl.semaphore_wait(zready.at[k - 1], 1)
            zcopy(k, UPPER).start()
            zcopy(k, LOWER).start()

    for h in (UPPER, LOWER):
        for k in (1, 3, 2):
            @pl.when(zh + k >= ZN)
            def _():
                zcopy(k, h).start()

    first = jnp.where(zh % 2 == 0, 3, 1)
    kinds = (0, first, 4 - first, 2)

    def ycopy(d, c, here, there, h):
        sign = 1 if d == RIGHT else -1
        piece = tall[h].at[slot(-sign * here, kinds[c])]
        src = piece
        return remote(
            src, piece, ys.at[d, there - 1, c, h], yr.at[d, there - 1, c, h], ypeer(sign * (there - here)), p
        )

    def along(c):
        return (UPPER,) if c in (1, 2) else (UPPER, LOWER)

    def await_piece(sem):
        pltpu.make_async_copy(tall_u.at[0], tall_u.at[0], sem).wait()

    near, far = (2, -2, 1, -1), (4, 3, -3)

    def bundle(k, planes, where):
        @pl.when(where)
        def _():
            for d in planes:
                piece = tall_l.at[slot(d, 0)]
                remote(piece, piece, bs.at[k // 2], br.at[k // 2], zpeer(k), p).start()

    def bundles(which):
        if which == "down":
            bundle(1, near, zh + 1 >= ZN)
            bundle(3, near, zh > 0)
        elif which == "up":
            bundle(1, near, zh + 1 < ZN)
            bundle(3, near, zh == 0)
        else:
            bundle(1, far, zh >= 0)
            bundle(3, far, zh >= 0)

    def bundle_wait(sem):
        size = (len(near) + len(far)) * part
        pltpu.make_async_copy(res.at[pl.ds(0, size), :], res.at[pl.ds(0, size), :], sem).wait()

    def onward(c, here, h):
        for d in (RIGHT, LEFT):
            for there in range(reach(d, c, h), here, -1):
                if here in (0, 2) and there <= here + 2:
                    ycopy(d, c, here, there, h).start()

    def zgot(c, h):
        await_piece(zr.at[kinds[c] - 1, h])
        if h in along(c):
            onward(c, 0, h)

    def ygot(c, here, h):
        for d in (RIGHT, LEFT):
            if here <= reach(d, c, h):
                await_piece(yr.at[d, here - 1, c, h])
        onward(c, here, h)

    onward(0, 0, LOWER)
    onward(0, 0, UPPER)

    def gcopy(i):
        j = turn(i, p)
        return j, remote(
            grad_ref.at[0, :, pl.ds(pl.multiple_of(j * blk, blk), blk)],
            gbuf.at[own_rows, :], gs.at[i], gr, g, owner_device(j),
        )

    for i in range(jn):
        j, copy = gcopy(i)

        @pl.when(owner_device(j) != p)
        def _():
            copy.start()

    @pl.when(active)
    def _():
        pltpu.make_async_copy(
            grad_ref.at[0, :, pl.ds(pl.multiple_of(mine * blk, blk), blk)], gbuf.at[own_rows, :], gr
        ).start()

    for load in loads[2:]:
        load.wait()
    layer = layer_ref[0]

    def prepare(n):
        part = slice(n * (blk // 4), (n + 1) * (blk // 4))

        @pl.when(active)
        def _():
            obt[:, part] = obuf[part, :].T
            spread = jnp.broadcast_to(ov_ref[...], (blk // 4, blk)).T
            values = iv_ref[:, pl.ds(pl.multiple_of(mine * blk + n * (blk // 4), blk // 4), blk // 4)]
            values = jnp.where(layer == 0, values[0:1], values[1:2])
            rbuf[:, part] = 1.0 / (spread * values + DAMPING)

    def project(n):
        lo, size = n * (blk // 4), blk // 4

        @pl.when(active)
        def _():
            if lo == 0:
                pltpu.make_async_copy(gbuf, gbuf, gr).wait()
            ybuf[lo : lo + size, :] = dot(obt[lo : lo + size, :], gbuf[...], ((1,), (0,))).astype(jnp.bfloat16)

    def tcopy(i, h):
        j = turn(i, p)
        return j, remote(tsend[h].at[j], tbuf.at[half_rows(h), :], ts.at[i, h], tr, g, owner_device(j))

    def owners(h):
        for i in range(jn):
            j, copy = tcopy(i, h)
            tsend[h][j] = tall[h][owner_ref[layer, j]]

            @pl.when(owner_device(j) != p)
            def _():
                copy.start()

        @pl.when(active)
        def _():
            pltpu.make_async_copy(tsend[h].at[mine], tbuf.at[half_rows(h), :], tr).start()

    for step in ORDER:
        what, n = step[0], step[1]
        if what == "up":
            zup(n, eval_where(step[2], zh))
        elif what == "z":
            zgot(n, step[2])
        elif what == "y":
            ygot(n, step[2], step[3])
        elif what == "bundle":
            bundles(n)
        elif what == "bundled":
            bundle_wait(br.at[n // 2])
        elif what == "prepare":
            prepare(n)
        elif what == "project":
            project(n)
        else:
            owners(n)

    def mcopy(dest):
        strip = pl.ds(pl.multiple_of(dest * rows, rows), rows)
        cols = pl.ds(pl.multiple_of(mine * blk, blk), blk)
        return res.at[strip, :], out_ref.at[0, :, cols]

    half = blk // 2
    parts = 2
    size, targets = blk // parts, pn // parts

    @pl.when(active)
    def _():
        pltpu.make_async_copy(tbuf, tbuf, tr).wait()
        for lo in (0, half):
            moments = dot(ybuf[lo : lo + half, :], tbuf[...], ((1,), (0,)))
            sbuf[lo : lo + half, :] = (moments * rbuf[lo : lo + half, :]).astype(jnp.bfloat16)
        for n in range(parts):
            turn = lax.rem(n + (p // 4 + 2) // (4 // parts), parts)
            part = pl.ds(pl.multiple_of(turn * size, size), size)
            mixed = dot(obuf[part, :], sbuf[...], ((1,), (0,))).astype(jnp.bfloat16)
            res[part, :] = dot(mixed, tbuf[...], ((1,), (1,))).astype(jnp.bfloat16)
            for i in sorted(range(targets), key=lambda i: i // 2 % 2):
                dest = turn * targets + i + 2 * (1 - p // 2 % 2) - 4 * (i // 2 % 2) * (1 - p // 2 % 2)
                src, dst = mcopy(dest)

                @pl.when(dest != p)
                def _():
                    remote(src, dst, ms.at[dest], mr, g, dest).start()

                @pl.when(dest == p)
                def _():
                    pltpu.make_async_copy(src, dst, mr).start()

    pltpu.make_async_copy(out_ref.at[0], out_ref.at[0], mr).wait()

    for h in (UPPER, LOWER):
        for k in (1, 2, 3):
            await_piece(zs.at[k - 1, h])
        for c in range(ZN):
            for d in (RIGHT, LEFT):
                for there in range(1, reach(d, c, h) + 1):
                    if h in along(c):
                        await_piece(ys.at[d, there - 1, c, h])
    for k in (1, 3):
        bundle_wait(bs.at[k // 2])
    for i in range(jn):
        j, copy = gcopy(i)

        @pl.when(owner_device(j) != p)
        def _():
            copy.wait_send()
            for h in (UPPER, LOWER):
                await_piece(ts.at[i, h])

    @pl.when(active)
    def _():
        for i in range(pn):
            src, dst = mcopy(i)

            @pl.when(i != p)
            def _():
                remote(src, dst, ms.at[i], mr, g, i).wait_send()


def solution(mesh):
    yn = mesh.shape["grad"] // ZN
    pn = mesh.shape["dp"]

    def shards(gradient, out_bases, in_bases, out_values, in_values, block_layer, in_owner):
        rows, width = gradient.shape[1:]
        blk = out_bases.shape[1]
        jn = width // blk
        slots = yn * ZN
        bf16, f32 = jnp.bfloat16, jnp.float32
        any_spec = pl.BlockSpec(memory_space=pl.ANY)
        vmem = pl.BlockSpec(memory_space=pltpu.VMEM)
        dma = pltpu.SemaphoreType.DMA

        def body(*refs):
            kernel(yn, pn, jn, *refs)

        return pl.pallas_call(
            body,
            out_shape=pltpu.VMEM(gradient.shape, bf16),
            in_specs=[any_spec] * 5 + [vmem] * 2,
            out_specs=vmem,
            scratch_shapes=[
                pltpu.SMEM(in_owner.shape, jnp.int32),
                pltpu.SMEM(block_layer.shape, jnp.int32),
                pltpu.VMEM((blk, blk), bf16),
                pltpu.VMEM((blk, blk), bf16),
                pltpu.VMEM((blk, blk), bf16),
                pltpu.VMEM((blk, blk), bf16),
                pltpu.VMEM((blk, blk), f32),
                pltpu.VMEM((slots, rows // 2, blk), bf16),
                pltpu.VMEM((slots, rows // 2, blk), bf16),
                pltpu.VMEM((jn, rows // 2, blk), bf16),
                pltpu.VMEM((jn, rows // 2, blk), bf16),
                pltpu.VMEM((blk, blk), bf16),
                pltpu.VMEM((blk, blk), bf16),
                pltpu.VMEM((blk, blk), bf16),
                dma((5,)),
                pltpu.SemaphoreType.REGULAR((ZN - 1,)),
                dma((ZN - 1, 2)),
                dma((ZN - 1, 2)),
                dma((2,)),
                dma((2,)),
                dma((2, 4, ZN, 2)),
                dma((2, 4, ZN, 2)),
                dma((jn,)),
                dma,
                dma((jn, 2)),
                dma,
                dma((pn,)),
                dma,
            ],
            compiler_params=pltpu.CompilerParams(
                collective_id=0, has_side_effects=True, vmem_limit_bytes=60 * 1024 * 1024
            ),
        )(in_owner, block_layer, gradient, out_bases, in_bases, out_values, in_values)

    in_specs = (
        P("grad", "dp", None),
        P("grad", None, None),
        P("grad", None, None),
        P("grad", None),
        P(),
        P("grad"),
        P(),
    )
    return jax.shard_map(shards, mesh=mesh, in_specs=in_specs, out_specs=P("grad", "dp", None), check_vma=False)
```

time: 47.8 us -> 44.4 us (0.929)
  Pallas kernels: 45.9 us -> 42.8 us
    pallas_call x1, Pallas kernels: 45.9 us -> 42.8 us  [shards(): pl.pallas_call(body, out_shape=pltpu.VMEM(gradient.shape, bf16), in_specs...]
where the time goes in v3:
time: 44.4 us; the launch traced here: 44.2 us
  Pallas kernels  42.8 us (96%)
  local copies, waits for them, and re-layouts  0.73 us (2%)
  between operations  0.66 us (1%)
    pallas_call x1, Pallas kernels, shards(): pl.pallas_call(body, out_shape=pltpu.VMEM(gradient.shape, bf16), in_specs...  42.8 us

profile of v3, /device:TPU:1, one launch (start us, length us, event | category | flops | bytes accessed | tf_op | source)
XLA Modules:
  0.0 44.2 jit_solution(17718062403262862668)
XLA Ops:
  0.7 42.8 %shard_map.73 = bf16[1,32,5120]{2,1,0:T(8,128)(2,1)S(1)} custom-call(s32[2,10]{1,0:T(2,128)} %refs_0_.1, s32[1]{0:T(128)S(6)} %copy.10.refs_1_, bf16[1,32,5120]{2,1,0:T(8,128)(2,1)} %refs_2_.1, bf16[1,512,512]{2,1,0:T(8,128)(2,1)} %refs_3_.1, bf16[1,512,512]{2,1,0:T(8,128)(2,1)} %refs_4_.1, f32[1,512]{1,0:T(1,128)} %refs_5_.1, f32[2,5120]{1,0:T(2,128)} %refs_6_.1), custom_call_target="tpu_custom_call" | custom-call | tf_op jit(solution)/shard_map/pallas_call | solution.py:361
  43.4 0.7 %copy.9 = bf16[1,32,5120]{2,1,0:T(8,128)(2,1)} copy(bf16[1,32,5120]{2,1,0:T(8,128)(2,1)S(1)} %shard_map.73) | data formatting | bytes 655360

commit v4 on v3

--- a/solution.py
+++ b/solution.py
@@ -56,9 +56,9 @@
 
 def kernel(
     yn, pn, jn,
-    owner_in, layer_in, grad_ref, ob_ref, ib_ref, ov_ref, iv_ref,
+    owner_in, layer_in, grad_ref, ob_ref, ib_ref, ov_in, iv_in,
     out_ref,
-    owner_ref, layer_ref, obuf, obt, gbuf, ybuf, rbuf, tall_u, tall_l, tsend_u, tsend_l, tbuf, sbuf, res,
+    owner_ref, layer_ref, ov_ref, iv_ref, obuf, obt, gbuf, ybuf, rbuf, tall_u, tall_l, tsend_u, tsend_l, tbuf, sbuf, res,
     lsem, zready, zs, zr, bs, br, ys, yr, gs, gr, ts, tr, ms, mr,
 ):
     g = lax.axis_index("grad")
@@ -95,6 +95,7 @@
             (
                 (ib_ref.at[0, half_rows(UPPER), :], tall_u.at[g]), (ib_ref.at[0, half_rows(LOWER), :], tall_l.at[g]),
                 (ob_ref.at[0], obuf), (owner_in, owner_ref), (layer_in, layer_ref),
+                (ov_in, ov_ref), (iv_in, iv_ref),
             )
         )
     ]
@@ -361,11 +362,13 @@
         return pl.pallas_call(
             body,
             out_shape=pltpu.VMEM(gradient.shape, bf16),
-            in_specs=[any_spec] * 5 + [vmem] * 2,
+            in_specs=[any_spec] * 7,
             out_specs=vmem,
             scratch_shapes=[
                 pltpu.SMEM(in_owner.shape, jnp.int32),
                 pltpu.SMEM(block_layer.shape, jnp.int32),
+                pltpu.VMEM(out_values.shape, f32),
+                pltpu.VMEM(in_values.shape, f32),
                 pltpu.VMEM((blk, blk), bf16),
                 pltpu.VMEM((blk, blk), bf16),
                 pltpu.VMEM((blk, blk), bf16),
@@ -378,7 +381,7 @@
                 pltpu.VMEM((blk, blk), bf16),
                 pltpu.VMEM((blk, blk), bf16),
                 pltpu.VMEM((blk, blk), bf16),
-                dma((5,)),
+                dma((7,)),
                 pltpu.SemaphoreType.REGULAR((ZN - 1,)),
                 dma((ZN - 1, 2)),
                 dma((ZN - 1, 2)),

time: 44.4 us -> 43.6 us (0.982)
  Pallas kernels: 42.8 us -> 42.1 us
    pallas_call x1, Pallas kernels: 42.8 us -> 42.1 us  [shards(): pl.pallas_call(body, out_shape=pltpu.VMEM(gradient.shape, bf16), in_specs...]
where the time goes in v4:
time: 43.6 us; the launch traced here: 43.5 us
  Pallas kernels  42.1 us (97%)
  local copies, waits for them, and re-layouts  0.73 us (2%)
  between operations  0.66 us (2%)
    pallas_call x1, Pallas kernels, shards(): pl.pallas_call(body, out_shape=pltpu.VMEM(gradient.shape, bf16), in_specs...  42.1 us

profile of v4, /device:TPU:1, one launch (start us, length us, event | category | flops | bytes accessed | tf_op | source)
XLA Modules:
  0.0 43.5 jit_solution(13745830052773264723)
XLA Ops:
  0.7 42.1 %shard_map.73 = bf16[1,32,5120]{2,1,0:T(8,128)(2,1)S(1)} custom-call(s32[2,10]{1,0:T(2,128)} %refs_0_.1, s32[1]{0:T(128)S(6)} %copy.10.refs_1_, bf16[1,32,5120]{2,1,0:T(8,128)(2,1)} %refs_2_.1, bf16[1,512,512]{2,1,0:T(8,128)(2,1)} %refs_3_.1, bf16[1,512,512]{2,1,0:T(8,128)(2,1)} %refs_4_.1, f32[1,512]{1,0:T(1,128)} %refs_5_.1, f32[2,5120]{1,0:T(2,128)} %refs_6_.1), custom_call_target="tpu_custom_call" | custom-call | tf_op jit(solution)/shard_map/pallas_call | solution.py:362
  42.7 0.7 %copy.9 = bf16[1,32,5120]{2,1,0:T(8,128)(2,1)} copy(bf16[1,32,5120]{2,1,0:T(8,128)(2,1)S(1)} %shard_map.73) | data formatting | bytes 655360

commit v5 on v4

--- a/solution.py
+++ b/solution.py
@@ -58,7 +58,7 @@
     yn, pn, jn,
     owner_in, layer_in, grad_ref, ob_ref, ib_ref, ov_in, iv_in,
     out_ref,
-    owner_ref, layer_ref, ov_ref, iv_ref, obuf, obt, gbuf, ybuf, rbuf, tall_u, tall_l, tsend_u, tsend_l, tbuf, sbuf, res,
+    owner_ref, layer_ref, ov_ref, iv_ref, obuf, obt, gbuf, ybuf, rbuf, xbuf, tall_u, tall_l, tsend_u, tsend_l, tbuf, sbuf, res,
     lsem, zready, zs, zr, bs, br, ys, yr, gs, gr, ts, tr, ms, mr,
 ):
     g = lax.axis_index("grad")
@@ -71,7 +71,7 @@
     tall, tsend = (tall_u, tall_l), (tsend_u, tsend_l)
 
     def half_rows(h):
-        return pl.ds(pl.multiple_of(p * rows + h * part, part), part)
+        return pl.ds(pl.multiple_of(h * (blk // 2) + p * part, part), part)
     active = (p % 2 == 1) | (p == 0) | (p == 10)
     mine = owned_block(p)
 
@@ -245,7 +245,7 @@
 
     def tcopy(i, h):
         j = turn(i, p)
-        return j, remote(tsend[h].at[j], tbuf.at[half_rows(h), :], ts.at[i, h], tr, g, owner_device(j))
+        return j, remote(tsend[h].at[j], tbuf.at[half_rows(h), :], ts.at[i, h], tr.at[h], g, owner_device(j))
 
     def owners(h):
         for i in range(jn):
@@ -258,7 +258,7 @@
 
         @pl.when(active)
         def _():
-            pltpu.make_async_copy(tsend[h].at[mine], tbuf.at[half_rows(h), :], tr).start()
+            pltpu.make_async_copy(tsend[h].at[mine], tbuf.at[half_rows(h), :], tr.at[h]).start()
 
     for step in ORDER:
         what, n = step[0], step[1]
@@ -290,10 +290,16 @@
 
     @pl.when(active)
     def _():
-        pltpu.make_async_copy(tbuf, tbuf, tr).wait()
-        for lo in (0, half):
-            moments = dot(ybuf[lo : lo + half, :], tbuf[...], ((1,), (0,)))
-            sbuf[lo : lo + half, :] = (moments * rbuf[lo : lo + half, :]).astype(jnp.bfloat16)
+        tops = [pl.ds(h * half, half) for h in (UPPER, LOWER)]
+        for h in (UPPER, LOWER):
+            pltpu.make_async_copy(tbuf.at[tops[h], :], tbuf.at[tops[h], :], tr.at[h]).wait()
+            for lo in (0, half):
+                some = slice(lo, lo + half)
+                product = dot(ybuf[some, tops[h]], tbuf[tops[h], :], ((1,), (0,)))
+                if h == UPPER:
+                    xbuf[some, :] = product
+                else:
+                    sbuf[some, :] = ((xbuf[some, :] + product) * rbuf[some, :]).astype(jnp.bfloat16)
         for n in range(parts):
             turn = lax.rem(n + (p // 4 + 2) // (4 // parts), parts)
             part = pl.ds(pl.multiple_of(turn * size, size), size)
@@ -374,6 +380,7 @@
                 pltpu.VMEM((blk, blk), bf16),
                 pltpu.VMEM((blk, blk), bf16),
                 pltpu.VMEM((blk, blk), f32),
+                pltpu.VMEM((blk, blk), f32),
                 pltpu.VMEM((slots, rows // 2, blk), bf16),
                 pltpu.VMEM((slots, rows // 2, blk), bf16),
                 pltpu.VMEM((jn, rows // 2, blk), bf16),
@@ -392,7 +399,7 @@
                 dma((jn,)),
                 dma,
                 dma((jn, 2)),
-                dma,
+                dma((2,)),
                 dma((pn,)),
                 dma,
             ],

time: 43.6 us -> 43.5 us (level)
  no operation moved by 1% of the time
where the time goes in v5:
time: 43.5 us; the launch traced here: 43.4 us
  Pallas kernels  42 us (97%)
  local copies, waits for them, and re-layouts  0.73 us (2%)
  between operations  0.66 us (2%)
    pallas_call x1, Pallas kernels, shards(): pl.pallas_call(body, out_shape=pltpu.VMEM(gradient.shape, bf16), in_specs...  42 us

profile of v5, /device:TPU:1, one launch (start us, length us, event | category | flops | bytes accessed | tf_op | source)
XLA Modules:
  0.0 43.4 jit_solution(5872527881364091708)
XLA Ops:
  0.7 42.0 %shard_map.73 = bf16[1,32,5120]{2,1,0:T(8,128)(2,1)S(1)} custom-call(s32[2,10]{1,0:T(2,128)} %refs_0_.1, s32[1]{0:T(128)S(6)} %copy.10.refs_1_, bf16[1,32,5120]{2,1,0:T(8,128)(2,1)} %refs_2_.1, bf16[1,512,512]{2,1,0:T(8,128)(2,1)} %refs_3_.1, bf16[1,512,512]{2,1,0:T(8,128)(2,1)} %refs_4_.1, f32[1,512]{1,0:T(1,128)} %refs_5_.1, f32[2,5120]{1,0:T(2,128)} %refs_6_.1), custom_call_target="tpu_custom_call" | custom-call | tf_op jit(solution)/shard_map/pallas_call | solution.py:368
  42.6 0.7 %copy.9 = bf16[1,32,5120]{2,1,0:T(8,128)(2,1)} copy(bf16[1,32,5120]{2,1,0:T(8,128)(2,1)S(1)} %shard_map.73) | data formatting | bytes 655360

commit v6 on v5

--- a/solution.py
+++ b/solution.py
@@ -18,9 +18,9 @@
     ("z", 2, UPPER), ("z", 3, UPPER), ("z", 3, LOWER), ("y", 0, 3, LOWER), ("y", 0, 4, LOWER), ("bundle", "far"),
     ("y", 1, 1, UPPER), ("y", 1, 2, UPPER), ("y", 2, 1, UPPER), ("y", 2, 2, UPPER), ("y", 3, 1, UPPER), ("y", 3, 2, UPPER),
     ("y", 3, 1, LOWER), ("y", 3, 2, LOWER),
-    ("y", 0, 3, UPPER), ("y", 0, 4, UPPER), ("y", 1, 3, UPPER), ("y", 1, 4, UPPER),
+    ("y", 1, 3, UPPER), ("y", 1, 4, UPPER),
     ("y", 2, 3, UPPER), ("y", 2, 4, UPPER), ("y", 3, 3, UPPER), ("y", 3, 4, UPPER),
-    ("owners", UPPER),
+    ("y", 0, 3, UPPER), ("y", 0, 4, UPPER), ("owners", UPPER),
     ("z", 1, LOWER), ("z", 2, LOWER), ("bundled", 1), ("bundled", 3), ("y", 3, 3, LOWER), ("y", 3, 4, LOWER),
     ("owners", LOWER), ("project", 0), ("project", 1), ("project", 2), ("project", 3),
 )
@@ -206,12 +206,14 @@
             gbuf.at[own_rows, :], gs.at[i], gr, g, owner_device(j),
         )
 
-    for i in range(jn):
-        j, copy = gcopy(i)
-
-        @pl.when(owner_device(j) != p)
-        def _():
-            copy.start()
+    for across in (True, False):
+        for i in range(jn):
+            j, copy = gcopy(i)
+            dest = owner_device(j)
+
+            @pl.when((dest != p) & ((dest // 2 % 2 != p // 2 % 2) == across))
+            def _():
+                copy.start()
 
     @pl.when(active)
     def _():
@@ -301,7 +303,7 @@
                 else:
                     sbuf[some, :] = ((xbuf[some, :] + product) * rbuf[some, :]).astype(jnp.bfloat16)
         for n in range(parts):
-            turn = lax.rem(n + (p // 4 + 2) // (4 // parts), parts)
+            turn = n
             part = pl.ds(pl.multiple_of(turn * size, size), size)
             mixed = dot(obuf[part, :], sbuf[...], ((1,), (0,))).astype(jnp.bfloat16)
             res[part, :] = dot(mixed, tbuf[...], ((1,), (1,))).astype(jnp.bfloat16)

time: 43.5 us -> 43.5 us (level)
  no operation moved by 1% of the time
where the time goes in v6:
time: 43.5 us; the launch traced here: 43.3 us
  Pallas kernels  41.9 us (96%)
  local copies, waits for them, and re-layouts  0.73 us (2%)
  between operations  0.66 us (2%)
    pallas_call x1, Pallas kernels, shards(): pl.pallas_call(body, out_shape=pltpu.VMEM(gradient.shape, bf16), in_specs...  41.9 us

profile of v6, /device:TPU:1, one launch (start us, length us, event | category | flops | bytes accessed | tf_op | source)
XLA Modules:
  0.0 43.3 jit_solution(11455171404472026293)
XLA Ops:
  0.7 41.9 %shard_map.73 = bf16[1,32,5120]{2,1,0:T(8,128)(2,1)S(1)} custom-call(s32[2,10]{1,0:T(2,128)} %refs_0_.1, s32[1]{0:T(128)S(6)} %copy.10.refs_1_, bf16[1,32,5120]{2,1,0:T(8,128)(2,1)} %refs_2_.1, bf16[1,512,512]{2,1,0:T(8,128)(2,1)} %refs_3_.1, bf16[1,512,512]{2,1,0:T(8,128)(2,1)} %refs_4_.1, f32[1,512]{1,0:T(1,128)} %refs_5_.1, f32[2,5120]{1,0:T(2,128)} %refs_6_.1), custom_call_target="tpu_custom_call" | custom-call | tf_op jit(solution)/shard_map/pallas_call | solution.py:370
  42.6 0.7 %copy.9 = bf16[1,32,5120]{2,1,0:T(8,128)(2,1)} copy(bf16[1,32,5120]{2,1,0:T(8,128)(2,1)S(1)} %shard_map.73) | data formatting | bytes 655360

commit v7 on v5

--- a/solution.py
+++ b/solution.py
@@ -27,19 +27,19 @@
 
 
 def owner_device(j):
-    return jnp.where(j < 8, 2 * j + 1, jnp.where(j == 8, 0, 10))
+    return jnp.where(j < 8, 2 * j + 1, jnp.where(j == 8, 8, 14))
 
 
 def turn(i, p):
     if i < 4:
         n = lax.rem(i + p // 2, 4)
-        return jnp.where(n == 0, 0, jnp.where(n == 1, 5, 6 + n))
+        return jnp.where(n == 0, 4, jnp.where(n == 1, 7, 6 + n))
     n = lax.rem(i - 4 + p // 2, 6)
-    return jnp.where(n < 4, n + 1, n + 2)
+    return n + (n >= 4).astype(jnp.int32) + (n >= 6).astype(jnp.int32)
 
 
 def owned_block(p):
-    return jnp.where(p % 2 == 1, p // 2, jnp.where(p == 0, 8, 9))
+    return jnp.where(p % 2 == 1, p // 2, jnp.where(p == 8, 8, 9))
 
 
 def reach(direction, c, h):
@@ -72,7 +72,7 @@
 
     def half_rows(h):
         return pl.ds(pl.multiple_of(h * (blk // 2) + p * part, part), part)
-    active = (p % 2 == 1) | (p == 0) | (p == 10)
+    active = (p % 2 == 1) | (p == 8) | (p == 14)
     mine = owned_block(p)
 
     def remote(src, dst, ssem, rsem, gg, pp):
@@ -301,12 +301,12 @@
                 else:
                     sbuf[some, :] = ((xbuf[some, :] + product) * rbuf[some, :]).astype(jnp.bfloat16)
         for n in range(parts):
-            turn = lax.rem(n + (p // 4 + 2) // (4 // parts), parts)
+            turn = n
             part = pl.ds(pl.multiple_of(turn * size, size), size)
             mixed = dot(obuf[part, :], sbuf[...], ((1,), (0,))).astype(jnp.bfloat16)
             res[part, :] = dot(mixed, tbuf[...], ((1,), (1,))).astype(jnp.bfloat16)
             for i in sorted(range(targets), key=lambda i: i // 2 % 2):
-                dest = turn * targets + i + 2 * (1 - p // 2 % 2) - 4 * (i // 2 % 2) * (1 - p // 2 % 2)
+                dest = turn * targets + i
                 src, dst = mcopy(dest)
 
                 @pl.when(dest != p)

time: 43.5 us -> 43.6 us (level)
  no operation moved by 1% of the time
where the time goes in v7:
time: 43.6 us; the launch traced here: 43.4 us
  Pallas kernels  42 us (96%)
  local copies, waits for them, and re-layouts  0.73 us (2%)
  between operations  0.66 us (2%)
    pallas_call x1, Pallas kernels, shards(): pl.pallas_call(body, out_shape=pltpu.VMEM(gradient.shape, bf16), in_specs...  42 us

profile of v7, /device:TPU:1, one launch (start us, length us, event | category | flops | bytes accessed | tf_op | source)
XLA Modules:
  0.0 43.4 jit_solution(5468741484406713790)
XLA Ops:
  0.7 42.0 %shard_map.73 = bf16[1,32,5120]{2,1,0:T(8,128)(2,1)S(1)} custom-call(s32[2,10]{1,0:T(2,128)} %refs_0_.1, s32[1]{0:T(128)S(6)} %copy.10.refs_1_, bf16[1,32,5120]{2,1,0:T(8,128)(2,1)} %refs_2_.1, bf16[1,512,512]{2,1,0:T(8,128)(2,1)} %refs_3_.1, bf16[1,512,512]{2,1,0:T(8,128)(2,1)} %refs_4_.1, f32[1,512]{1,0:T(1,128)} %refs_5_.1, f32[2,5120]{1,0:T(2,128)} %refs_6_.1), custom_call_target="tpu_custom_call" | custom-call | tf_op jit(solution)/shard_map/pallas_call | solution.py:368
  42.7 0.7 %copy.9 = bf16[1,32,5120]{2,1,0:T(8,128)(2,1)} copy(bf16[1,32,5120]{2,1,0:T(8,128)(2,1)S(1)} %shard_map.73) | data formatting | bytes 655360
